TPU v7x, 32 devices: a whole 2x2x4 slice. The times are simulated.
32 devices in a mesh: seq: 16 (over z, x, core), mp: 2 (over y).
Axes of the slice: x: 2, y: 2, z: 4, core: 2. Of those that a mesh axis runs over, the one named last changes fastest.
Arguments:
- q_new: bfloat16 [4096, 3072], P('seq', 'mp'), may hold values from -100 to 100
- k_new: bfloat16 [4096, 3072], P('seq', 'mp'), may hold values from -100 to 100
- v_new: bfloat16 [4096, 3072], P('seq', 'mp'), may hold values from -6 to 6
- q_gain: float32 [3072], P('mp'), may hold values from 0.1 to 1.9
- k_gain: float32 [3072], P('mp'), may hold values from 0.1 to 1.9
- cache_k: bfloat16 [256, 128, 3072], P('seq', None, 'mp'), may hold values from -300 to 300
- cache_v: bfloat16 [256, 128, 3072], P('seq', None, 'mp'), may hold values from -6 to 6
- new_count: int32 [16, 2], replicated, may hold values from 1 to 192, 256 in all within a row
- prefix_blocks: int32 [32], replicated, may hold values from 0 to 16, as said below
- block_req: int32 [256], replicated, may hold values from 0 to 31, as said below
Outputs:
- attended: bfloat16 [4096, 3072], P('seq', 'mp')
Inputs may be any that keep to these rules, and one draw needn't show every extreme that they name: Pool rows s * 16 .. (s + 1) * 16 - 1 lie on index s of seq; these blocks belong to requests of 16 different indices of seq (block_req // 2); exactly one request, the same on every index, owns one block on every index of seq (16 blocks in all). prefix_blocks[r] is the number of pool blocks b with block_req[b] = r.
All inputs are finite; a program needn't handle non-finite values.
Results may differ from a plain program's by a relative error of at most 0.015.
Values may be sent and summed in bfloat16 or wider, within the bound.
A program may use at most 128 MiB of HBM per device.

v0:
```python
import jax
import jax.numpy as jnp
from jax import lax
from jax.sharding import PartitionSpec as P

HD = 128


NEGATIVE = -1e30


def rotate(field, position):
    half = field.shape[-1] // 2
    freq = 500000.0 ** (-(jnp.arange(half, dtype=jnp.float32) / half))
    angle = position.astype(jnp.float32)[:, None] * freq[None, :]
    cosine = jnp.cos(angle)[:, None, :]
    sine = jnp.sin(angle)[:, None, :]
    first = field[..., :half]
    second = field[..., half:]
    return jnp.concatenate([first * cosine - second * sine, second * cosine + first * sine], -1)


def token_meta(counts, prefix, first_req, block_len, tokens_here):
    cumul = jnp.cumsum(counts, axis=1)
    starts = cumul - counts
    order = jnp.arange(tokens_here, dtype=jnp.int32)
    local = jnp.sum((order[None, :, None] >= cumul[:, None, :]).astype(jnp.int32), -1)
    picker = (
        local[:, :, None] == jnp.arange(counts.shape[1], dtype=jnp.int32)[None, None, :]
    ).astype(jnp.int32)
    offset = order[None, :] - jnp.sum(picker * starts[:, None, :], -1)
    before = jnp.sum(picker * prefix[:, None, :], -1)
    return (first_req[:, None] + local, before * block_len + offset)


def update(carry, queries, keys_in, values_in, query_req, key_req):
    best, total, accum = carry
    scores = jnp.einsum(
        "thd,khd->htk", queries, keys_in, preferred_element_type=jnp.float32
    ) * queries.shape[-1] ** (-0.5)
    allowed = (query_req[:, None] == key_req[None, :])[None]
    scores = jnp.where(allowed, scores, NEGATIVE)
    fresh = jnp.maximum(best, jnp.max(scores, -1))
    weights = jnp.where(allowed, jnp.exp(scores - fresh[..., None]), 0.0)
    factor = jnp.exp(best - fresh)
    total = total * factor + jnp.sum(weights, -1)
    accum = accum * factor[..., None] + jnp.einsum(
        "htk,khd->htd", weights.astype(jnp.bfloat16), values_in, preferred_element_type=jnp.float32
    )
    return (fresh, total, accum)


def guarded(carry, queries, keys_in, values_in, query_req, key_req):
    return update(carry, queries, keys_in, values_in, query_req, key_req)


def shards(
    q_new, k_new, v_new, q_gain, k_gain, cache_k, cache_v, new_count, prefix_blocks, block_req
):
    tokens_here = q_new.shape[0]
    width_all = q_new.shape[1] * lax.axis_size("mp")
    heads_here = q_new.shape[1] // HD
    block_len = cache_k.shape[1]
    blocks_here = cache_k.shape[0]
    slots = lax.axis_size("seq")
    device = lax.axis_index("seq")
    per_dev = new_count.shape[1]
    query_f = q_new.astype(jnp.float32)
    key_f = k_new.astype(jnp.float32)
    square_q, square_k = lax.psum(
        (jnp.sum(query_f * query_f, -1), jnp.sum(key_f * key_f, -1)), "mp"
    )
    first_all = jnp.arange(slots, dtype=jnp.int32) * per_dev
    req_all, pos_all = token_meta(
        new_count, prefix_blocks.reshape(slots, per_dev), first_all, block_len, tokens_here
    )
    query_req = lax.dynamic_index_in_dim(req_all, device, 0, keepdims=False)
    position = lax.dynamic_index_in_dim(pos_all, device, 0, keepdims=False)
    normed_q = query_f * lax.rsqrt(square_q / width_all + 1e-06)[:, None] * q_gain
    normed_k = key_f * lax.rsqrt(square_k / width_all + 1e-06)[:, None] * k_gain
    queries = rotate(normed_q.reshape(tokens_here, heads_here, HD), position).astype(jnp.bfloat16)
    keys_here = rotate(normed_k.reshape(tokens_here, heads_here, HD), position).astype(jnp.bfloat16)
    values_here = v_new.reshape(tokens_here, heads_here, HD)
    scores = jnp.einsum(
        "thd,shd->hts", queries, keys_here, preferred_element_type=jnp.float32
    ) * HD ** (-0.5)
    order = jnp.arange(tokens_here, dtype=jnp.int32)
    allowed = (query_req[:, None] == query_req[None, :]) & (order[:, None] >= order[None, :])
    scores = jnp.where(allowed[None], scores, NEGATIVE)
    best = jnp.max(scores, -1)
    weights = jnp.where(allowed[None], jnp.exp(scores - best[..., None]), 0.0)
    total = jnp.sum(weights, -1)
    accum = jnp.einsum(
        "hts,shd->htd",
        weights.astype(jnp.bfloat16),
        values_here,
        preferred_element_type=jnp.float32,
    )
    carry = (best, total, accum)
    owner_table = block_req.reshape(slots, blocks_here)
    dest_table = owner_table // per_dev
    targets = jnp.arange(slots, dtype=jnp.int32)
    mine = lax.dynamic_index_in_dim(dest_table, device, 0, keepdims=False)
    hit = mine[None, :] == targets[:, None]
    arrive = dest_table == device
    picks = jnp.sum(jnp.where(hit, jnp.arange(blocks_here, dtype=jnp.int32)[None, :], 0), 1)
    present = jnp.any(hit, 1)[:, None, None]
    send_keys = jnp.where(present, jnp.take(cache_k, picks, axis=0), jnp.zeros((), jnp.bfloat16))
    send_values = jnp.where(present, jnp.take(cache_v, picks, axis=0), jnp.zeros((), jnp.bfloat16))
    got_keys, got_values = (
        lax.all_to_all(send_keys, "seq", split_axis=0, concat_axis=0, tiled=True),
        lax.all_to_all(send_values, "seq", split_axis=0, concat_axis=0, tiled=True),
    )
    slot_req = jnp.where(jnp.any(arrive, 1), jnp.sum(jnp.where(arrive, owner_table, 0), 1), -1)
    group = 8
    rounds = slots // group
    keys_all = got_keys.reshape(rounds, group * block_len, heads_here, HD)
    values_all = got_values.reshape(rounds, group * block_len, heads_here, HD)
    owners_all = jnp.repeat(slot_req, block_len).reshape(rounds, group * block_len)

    def visit(state, item):
        group_keys, group_values, group_req = item
        return (guarded(state, queries, group_keys, group_values, query_req, group_req), None)

    carry, _ = lax.scan(visit, carry, (keys_all, values_all, owners_all))
    best, total, accum = carry
    result = (accum / total[..., None]).astype(jnp.bfloat16)
    return jnp.transpose(result, (1, 0, 2)).reshape(tokens_here, heads_here * HD)


def solution(mesh):
    return jax.shard_map(
        shards,
        mesh=mesh,
        in_specs=(
            P("seq", "mp"),
            P("seq", "mp"),
            P("seq", "mp"),
            P("mp"),
            P("mp"),
            P("seq", None, "mp"),
            P("seq", None, "mp"),
            P(),
            P(),
            P(),
        ),
        out_specs=P("seq", "mp"),
        check_vma=False,
    )
```

profile of v0, /device:TPU:11, one launch (start us, length us, event | category | flops | bytes accessed | tf_op | source)
XLA Modules:
  0.0 355.5 jit_solution(13228140350335104269)
XLA Ops:
  0.0 0.8 reshape.183
  0.8 0.1 select_reduce_fusion.3
  1.0 0.1 fusion.40
  1.2 6.4 %gather_fusion = bf16[16,128,1536]{2,1,0:T(8,128)(2,1)} fusion(bf16[16,128,1536]{2,1,0:T(8,128)(2,1)} %param.19, s32[1024]{0:T(1024)S(1)} %pad_clamp_fusion), kind=kCustom, calls=%fused_computation.clone | custom fusion | bytes 12582976 | tf_op jit(solution)/shard_map/jit(_take)/gather | solution.py:108
  7.6 6.4 %gather_fusion.1 = bf16[16,128,1536]{2,1,0:T(8,128)(2,1)} fusion(bf16[16,128,1536]{2,1,0:T(8,128)(2,1)} %param.20, s32[1024]{0:T(1024)S(1)} %pad_clamp_fusion), kind=kCustom, calls=%fused_computation.1.clone | custom fusion | bytes 12582976 | tf_op jit(solution)/shard_map/jit(_take)/gather | solution.py:109
  13.9 8.6 %select_select_fusion = (bf16[16,128,1536]{2,1,0:T(8,128)(2,1)}, bf16[16,128,1536]{2,1,0:T(8,128)(2,1)S(1)}) fusion(bf16[16,128,1536]{2,1,0:T(8,128)(2,1)} %gather_fusion.1, pred[16]{0:T(512)(128)(4,1)S(1)} %compare_and_fusion, pred[16]{0:T(512)(128)(4,1)S(1)} %fusion.40, bf16[16,128,1536]{2,1,0:T(8,128)(2,1)} %gather_fusion), kind=kLoop, calls=%fused_computation.24 | loop fusion | flops 12582912 | bytes 25165856 | tf_op jit(solution)/shard_map/jit(_where)/select_n | solution.py:109
  22.6 143.6 %all_to_all.10 = bf16[16,128,1536]{2,1,0:T(8,128)(2,1)} all-to-all(bf16[16,128,1536]{2,1,0:T(8,128)(2,1)S(1)} %get-tuple-element.116), channel_id=1, replica_groups=mesh['seq'=16,'mp'=2] {'seq'}, dimensions={0} | all-to-all | bytes 12582912 | tf_op jit(solution)/shard_map/all_to_all | solution.py:111
  166.2 5.7 %all-to-all-start.1 = ((bf16[16,128,1536]{2,1,0:T(8,128)(2,1)}), bf16[16,128,1536]{2,1,0:T(8,128)(2,1)}, u32[]{:S(2)}, u32[]{:S(2)}) async-start(bf16[16,128,1536]{2,1,0:T(8,128)(2,1)} %get-tuple-element.115), calls=%async_computation.1 | async-start | bytes 12582912 | tf_op jit(solution)/shard_map/all_to_all | solution.py:112
  172.1 0.3 copy.36
  172.4 0.3 copy.40
  172.7 0.2 fusion.23
  172.9 0.2 fusion.25
  173.1 4.4 %all-reduce = (f32[256]{0:T(256)S(1)}, f32[256]{0:T(256)S(1)}) all-reduce(f32[256]{0:T(256)S(1)} %fusion.23, f32[256]{0:T(256)S(1)} %fusion.25), channel_id=1, replica_groups=mesh['seq'=16,'mp'=2] {'mp'}, use_global_device_ids=true, to_apply=%region_3.0 | all-reduce | flops 512 | bytes 4096 | tf_op jit(solution)/shard_map/psum | solution.py:70
  177.5 0.3 fusion.24
  177.8 1.0 fusion.50
  178.8 1.6 copy.59
  180.4 1.6 copy.60
  182.1 0.3 fusion.26
  182.3 0.1 fusion.49
  182.5 1.6 copy.61
  184.1 1.6 copy.62
  185.7 0.6 dynamic-slice
  186.3 2.3 copy.43
  188.6 0.1 reduce_or.18
  189.0 0.6 dynamic-slice_add_fusion
  189.6 0.5 multiply_cosine_fusion
  190.2 3.2 subtract_convert_fusion
  193.4 0.4 pad_maximum_fusion
  194.0 0.9 fusion.20
  194.9 0.8 fusion.22
  195.7 1.1 fusion.27
  196.7 12.2 %reshape.209 = bf16[2,1024,12,128]{3,2,1,0:T(8,128)(2,1)} reshape(bf16[16,128,1536]{2,1,0:T(8,128)(2,1)} %all_to_all.10) | data formatting | bytes 12582912 | tf_op jit(solution)/shard_map/reshape | solution.py:117
  208.9 7.6 %copy.48 = bf16[2,1024,12,128]{3,1,2,0:T(8,128)(2,1)} copy(bf16[2,1024,12,128]{3,2,1,0:T(8,128)(2,1)} %reshape.209) | data formatting | bytes 12582912 | tf_op jit(solution)/shard_map/while | solution.py:125
  216.5 92.8 %all-to-all-done.1 = bf16[16,128,1536]{2,1,0:T(8,128)(2,1)} async-done(((bf16[16,128,1536]{2,1,0:T(8,128)(2,1)}), bf16[16,128,1536]{2,1,0:T(8,128)(2,1)}, u32[]{:S(2)}, u32[]{:S(2)}) %all-to-all-start.1) | async-done | bytes 6291488 | tf_op jit(solution)/shard_map/all_to_all | solution.py:112
  309.3 12.2 %reshape.210 = bf16[2,1024,12,128]{3,2,1,0:T(8,128)(2,1)} reshape(bf16[16,128,1536]{2,1,0:T(8,128)(2,1)} %all-to-all-done.1) | data formatting | bytes 12582912 | tf_op jit(solution)/shard_map/reshape | solution.py:118
  321.4 7.7 %copy.49 = bf16[2,1024,12,128]{3,1,2,0:T(8,128)(2,1)} copy(bf16[2,1024,12,128]{3,2,1,0:T(8,128)(2,1)} %reshape.210) | data formatting | bytes 12582912 | tf_op jit(solution)/shard_map/while | solution.py:125
  329.1 24.5 %while.14 = (s32[]{:T(128)}, f32[12,256]{1,0:T(8,128)S(1)}, f32[12,256]{1,0:T(8,128)S(1)}, f32[12,256,128]{2,1,0:T(8,128)S(1)}, s32[256]{0:T(256)S(1)}, /*index=...) while((s32[]{:T(128)}, f32[12,256]{1,0:T(8,128)S(1)}, ...), condition=%wide.region_17.19_spmd, body=%wide.region_14.18_spmd.sunk | while | flops 1652561920 | bytes 74405512 | solution.py:125
  329.2 0.2 broadcast_compare_fusion.4
  329.4 3.9 %fusion.62 = (f32[12,256]{1,0:T(8,128)S(1)}, f32[12,1024,256]{2,1,0:T(8,128)S(1)}) fusion(pred[256,1024]{0,1:T(8,128)(4,1)S(1)} %broadcast_compare_fusion.4, bf16[256,12,128]{2,0,1:T(8,128)(2,1)S(1)} %get-tuple-element.211, bf16[2,1024,12,128]{3,1,2,0:T(8,128)(2,1)} %get-tuple-element.210, s32[]{:T(128)} %get-tuple-element.194), kind=kOutput, calls=%fused_computation.4.clone.1 | convolution fusion | flops 814740480 | bytes 16790016 | tf_op jit(solution)/shard_map/while/body/eval_jaxpr/thd,khd->htk/dot_general | solution.py:38
  333.3 3.1 fusion.63
  336.5 4.9 %multiply_add_fusion.5 = f32[12,256,128]{2,1,0:T(8,128)S(1)} fusion(f32[12,256,128]{2,1,0:T(8,128)S(1)} %get-tuple-element.197, bf16[2,1024,12,128]{3,1,2,0:T(8,128)(2,1)S(1)} %copy-done, s32[]{:T(128)} %get-tuple-element.194, f32[12,1024,256]{2,1,0:T(8,128)S(1)} %get-tuple-element.181, f32[12,256]{1,0:T(8,128)S(1)} %max.4, ...), kind=kOutput, calls=%fused_computation.14.clone.1 | convolution fusion | flops 821821440 | bytes 19169284 | tf_op jit(solution)/shard_map/while/body/eval_jaxpr/htk,khd->htd/dot_general | solution.py:47
  341.4 0.2 broadcast_compare_fusion.4
  341.6 3.9 %fusion.62 = (f32[12,256]{1,0:T(8,128)S(1)}, f32[12,1024,256]{2,1,0:T(8,128)S(1)}) fusion(pred[256,1024]{0,1:T(8,128)(4,1)S(1)} %broadcast_compare_fusion.4, bf16[256,12,128]{2,0,1:T(8,128)(2,1)S(1)} %get-tuple-element.211, bf16[2,1024,12,128]{3,1,2,0:T(8,128)(2,1)} %get-tuple-element.210, s32[]{:T(128)} %get-tuple-element.194), kind=kOutput, calls=%fused_computation.4.clone.1 | convolution fusion | flops 814740480 | bytes 16790016 | tf_op jit(solution)/shard_map/while/body/eval_jaxpr/thd,khd->htk/dot_general | solution.py:38
  345.6 3.1 fusion.63
  348.7 4.9 %multiply_add_fusion.5 = f32[12,256,128]{2,1,0:T(8,128)S(1)} fusion(f32[12,256,128]{2,1,0:T(8,128)S(1)} %get-tuple-element.197, bf16[2,1024,12,128]{3,1,2,0:T(8,128)(2,1)S(1)} %copy-done, s32[]{:T(128)} %get-tuple-element.194, f32[12,1024,256]{2,1,0:T(8,128)S(1)} %get-tuple-element.181, f32[12,256]{1,0:T(8,128)S(1)} %max.4, ...), kind=kOutput, calls=%fused_computation.14.clone.1 | convolution fusion | flops 821821440 | bytes 19169284 | tf_op jit(solution)/shard_map/while/body/eval_jaxpr/htk,khd->htd/dot_general | solution.py:47
  353.6 0.5 copy.50
  354.1 0.2 divide_convert_fusion
  354.3 1.2 copy.51
  (46 shorter events, 0.9 us)
Async XLA Ops:
  166.2 5.7 %copy-start.6 = (s32[16,2]{0,1:T(2,128)S(1)}, s32[16,2]{0,1:T(2,128)}, u32[]{:S(2)}) copy-start(s32[16,2]{0,1:T(2,128)} %param.21) | copy-start | bytes 388
  166.2 5.7 %copy-start.7 = (s32[32]{0:T(128)S(1)}, s32[32]{0:T(128)}, u32[]{:S(2)}) copy-start(s32[32]{0:T(128)} %param.22) | copy-start | bytes 388
  166.2 5.9 %copy-start.1 = (bf16[256,1536]{1,0:T(8,128)(2,1)S(1)}, bf16[256,1536]{1,0:T(8,128)(2,1)}, u32[]{:S(2)}) copy-start(bf16[256,1536]{1,0:T(8,128)(2,1)} %param.14) | copy-start | bytes 2359300
  166.2 6.2 %copy-start.2 = (bf16[256,1536]{1,0:T(8,128)(2,1)S(1)}, bf16[256,1536]{1,0:T(8,128)(2,1)}, u32[]{:S(2)}) copy-start(bf16[256,1536]{1,0:T(8,128)(2,1)} %param.15) | copy-start | bytes 2359300
  166.2 143.1 %all-to-all-start.1 = ((bf16[16,128,1536]{2,1,0:T(8,128)(2,1)}), bf16[16,128,1536]{2,1,0:T(8,128)(2,1)}, u32[]{:S(2)}, u32[]{:S(2)}) async-start(bf16[16,128,1536]{2,1,0:T(8,128)(2,1)} %get-tuple-element.115), calls=%async_computation.1 | async-start | bytes 12582912 | tf_op jit(solution)/shard_map/all_to_all | solution.py:112
  171.9 5.6 %copy-start.4 = (f32[1536]{0:T(1024)S(1)}, f32[1536]{0:T(1024)}, u32[]{:S(2)}) copy-start(f32[1536]{0:T(1024)} %param.17) | copy-start | bytes 18436
  178.8 3.2 copy-start.5
  194.0 1.7 copy-start.3
  333.3 3.2 copy-start
  345.5 3.2 copy-start
where the time goes:
time: 357 us; the launch traced here: 355 us
  blocking collectives  148 us (41%)
  waiting for transfers between devices  92.8 us (26%)
  local copies, waits for them, and re-layouts  66.2 us (19%)
  other arithmetic  22.9 us (6%)
  matrix products  19.5 us (5%)
  starting transfers between devices  5.65 us (2%)
    all_to_all x1, blocking collectives, shards(): lax.all_to_all(send_keys, 'seq', split_axis=0, concat_axis=0, tiled=True)  144 us
    all_to_all x1, waiting for transfers between devices, shards(): lax.all_to_all(send_values, 'seq', split_axis=0, concat_axis=0, tiled=True)  92.8 us
    while x3, local copies, waits for them, and re-layouts, shards(): carry, _ = lax.scan(visit, carry, (keys_all, values_all, owners_all))  15.7 us
    reshape x1, local copies, waits for them, and re-layouts, shards(): keys_all = got_keys.reshape(rounds, group * block_len, heads_here, HD)  12.2 us
    reshape x1, local copies, waits for them, and re-layouts, shards(): values_all = got_values.reshape(rounds, group * block_len, heads_here, HD)  12.2 us
    dot_general x2, matrix products, update(): jnp.einsum('htk,khd->htd', weights.astype(jnp.bfloat16), values_in, prefe...  9.78 us
    unnamed x23, local copies, waits for them, and re-layouts  9.43 us
    select_n x1, other arithmetic, shards(): jnp.where(present, jnp.take(cache_v, picks, axis=0), jnp.zeros((), jnp.bf...  8.61 us
  transfers between devices with their start and end apart: 1, of which 1 were waited for; matrix products, arithmetic and copies ran while one was open for 11% of the time, Pallas kernels for 0%

commit v1 on v0

v1 whole, which is shorter than its diff:
```python
import functools

import jax
import jax.numpy as jnp
from jax import lax
from jax.experimental import pallas as pl
from jax.experimental.pallas import tpu as pltpu
from jax.sharding import PartitionSpec as P

HD = 128
NEGATIVE = -1e30
LOG2E = 1.4426950408889634
MAJOR = 4
VMEM_LIMIT = 62 * 1024 * 1024


def rotate(field, position):
    half = field.shape[-1] // 2
    freq = 500000.0 ** (-(jnp.arange(half, dtype=jnp.float32) / half))
    angle = position.astype(jnp.float32)[:, None] * freq[None, :]
    cosine = jnp.cos(angle)[:, None, :]
    sine = jnp.sin(angle)[:, None, :]
    first = field[..., :half]
    second = field[..., half:]
    return jnp.concatenate([first * cosine - second * sine, second * cosine + first * sine], -1)


def kernel(
    A, B, H, G,
    table, q_ref, k_ref, v_ref, row_req, col_req, ck_hbm, cv_hbm,
    out_ref,
    qall, kc, vc, part, stat, cpart, cstat, xpart, xstat, zpart, zstat, lacc, lstat,
    kv_sem, agz_s, agz_r, agx_s, agx_r, agc_s, agc_r,
    cp_s, cp_r, cs_s, cs_r, xp_s, xp_r, xs_s, xs_r, zp_s, zp_r, zs_s, zs_r,
):
    me = lax.axis_index("seq")
    T = q_ref.shape[1]
    core = lax.rem(me, 2)
    minor = lax.rem(me // 2, B)
    major = me // (2 * B)
    scale = HD ** (-0.5) * LOG2E

    def at(a, b):
        return (lax.rem(major + a + A, A) * B + lax.rem(minor + b + B, B)) * 2 + core

    sibling = me + 1 - 2 * core

    def slot(a, b, c):
        return (a * B + b) * 2 + c

    def remote(src, dst, send, recv, where):
        return pltpu.make_async_remote_copy(
            src_ref=src, dst_ref=dst, send_sem=send, recv_sem=recv,
            device_id={"seq": where}, device_id_type=pl.DeviceIdType.MESH,
        )

    def agz(a):
        return remote(qall.at[0], qall.at[slot(a, 0, 0)], agz_s.at[a], agz_r.at[a], at(-a, 0))

    def agx(a, b):
        i = a * B + b
        return remote(qall.at[slot(a, 0, 0)], qall.at[slot(a, b, 0)], agx_s.at[i], agx_r.at[i], at(0, -b))

    def agc(a, b):
        i = a * B + b
        return remote(qall.at[slot(a, b, 0)], qall.at[slot(a, b, 1)], agc_s.at[i], agc_r.at[i], sibling)

    def rsc(a, b):
        i = a * B + b
        return (
            remote(part.at[slot(a, b, 1)], cpart.at[i], cp_s.at[i], cp_r.at[i], sibling),
            remote(stat.at[slot(a, b, 1)], cstat.at[i], cs_s.at[i], cs_r.at[i], sibling),
        )

    def rsx(a, b):
        i = a * (B - 1) + b - 1
        return (
            remote(part.at[slot(a, b, 0)], xpart.at[i], xp_s.at[i], xp_r.at[i], at(0, b)),
            remote(stat.at[slot(a, b, 0)], xstat.at[i], xs_s.at[i], xs_r.at[i], at(0, b)),
        )

    def rsz(a):
        i = a - 1
        return (
            remote(part.at[slot(a, 0, 0)], zpart.at[i], zp_s.at[i], zp_r.at[i], at(a, 0)),
            remote(stat.at[slot(a, 0, 0)], zstat.at[i], zs_s.at[i], zs_r.at[i], at(a, 0)),
        )

    def start(copies):
        for copy in copies:
            copy.start()

    def arrived(copies):
        for copy in copies:
            copy.wait_recv()

    def sent(copies):
        for copy in copies:
            copy.wait_send()

    def each_b(body):
        if B == 2:
            body(1)
        else:
            lax.fori_loop(1, B, lambda b, _: (body(b), 0)[1], 0)

    copies = [
        pltpu.make_async_copy(ck_hbm, kc, kv_sem.at[0]),
        pltpu.make_async_copy(cv_hbm, vc, kv_sem.at[1]),
    ]
    start(copies)
    qall[0] = q_ref[...]

    barrier = pltpu.get_barrier_semaphore()

    def greet(where):
        pl.semaphore_signal(barrier, inc=1, device_id={"seq": where}, device_id_type=pl.DeviceIdType.MESH)

    greet(sibling)
    for a in range(1, A):
        greet(at(a, 0))
    each_b(lambda b: greet(at(0, b)))
    pl.semaphore_wait(barrier, 1 + (A - 1) + (B - 1))

    def forward(a):
        each_b(lambda b: agx(a, b).start())
        agc(a, 0).start()

    for a in range(1, A):
        agz(a).start()
    forward(0)

    def cols(h):
        return pl.ds(pl.multiple_of(h * HD, HD), HD)

    def heads(body):
        def group(g, _):
            for j in range(G):
                body(g * G + j)
            return 0

        lax.fori_loop(0, H // G, group, 0)

    def local(h):
        s = jnp.dot(k_ref[:, cols(h)], q_ref[cols(h), :], preferred_element_type=jnp.float32)
        order_s = lax.broadcasted_iota(jnp.int32, (T, T), 0)
        order_t = lax.broadcasted_iota(jnp.int32, (T, T), 1)
        allowed = (col_req[...] == row_req[...]) & (order_s <= order_t)
        s = jnp.where(allowed, s, NEGATIVE)
        m = jnp.max(s, 0, keepdims=True)
        p = jnp.exp2((s - m) * scale)
        lstat[pl.ds(h, 1), :] = m
        lstat[pl.ds(H + h, 1), :] = jnp.sum(p, 0, keepdims=True)
        lacc[cols(h), :] = lax.dot_general(
            v_ref[:, cols(h)], p.astype(jnp.bfloat16), (((0,), (0,)), ((), ())),
            preferred_element_type=jnp.float32,
        )

    heads(local)
    for copy in copies:
        copy.wait()

    def compute(i):
        pick = table[0, i]
        token = lax.broadcasted_iota(jnp.int32, (1, T), 1)
        match = (token >= table[1, i]) & (token < table[2, i])

        def one(h):
            k = kc[pick, :, cols(h)]
            v = vc[pick, :, cols(h)]
            s = jnp.dot(k, qall[i, cols(h), :], preferred_element_type=jnp.float32)
            m = jnp.max(s, 0, keepdims=True)
            p = jnp.exp2((s - m) * scale)
            stat[i, pl.ds(h, 1), :] = jnp.where(match, m, NEGATIVE)
            stat[i, pl.ds(H + h, 1), :] = jnp.sum(p, 0, keepdims=True)
            acc = lax.dot_general(
                v, p.astype(jnp.bfloat16), (((0,), (0,)), ((), ())), preferred_element_type=jnp.float32
            )
            part[i, cols(h), :] = acc.astype(jnp.bfloat16)

        heads(one)

    def merge(i, other, ostat, j):
        def one(h):
            m1, m2 = stat[i, pl.ds(h, 1), :], ostat[j, pl.ds(h, 1), :]
            m = jnp.maximum(m1, m2)
            f1, f2 = jnp.exp2((m1 - m) * scale), jnp.exp2((m2 - m) * scale)
            stat[i, pl.ds(h, 1), :] = m
            stat[i, pl.ds(H + h, 1), :] = (
                stat[i, pl.ds(H + h, 1), :] * f1 + ostat[j, pl.ds(H + h, 1), :] * f2
            )
            part[i, cols(h), :] = (
                part[i, cols(h), :].astype(jnp.float32) * f1 + other[j, cols(h), :].astype(jnp.float32) * f2
            ).astype(jnp.bfloat16)

        heads(one)

    def unit(a, b):
        agc(a, b).wait_recv()
        compute(slot(a, b, 1))
        start(rsc(a, b))
        compute(slot(a, b, 0))

    def merge_core(a, b):
        arrived(rsc(a, b))
        merge(slot(a, b, 0), cpart, cstat, a * B + b)

    def merge_minor(a):
        def body(b):
            arrived(rsx(a, b))
            merge(slot(a, 0, 0), xpart, xstat, a * (B - 1) + b - 1)

        each_b(body)

    for a in range(A):
        unit(a, 0)
        if a + 1 < A:
            agz(a + 1).wait_recv()
            forward(a + 1)

        def far(b, a=a):
            agx(a, b).wait_recv()
            agc(a, b).start()
            unit(a, b)

        each_b(far)

        def near(b, a=a):
            merge_core(a, b)
            if a > 0:
                start(rsx(a, b))

        each_b(near)
        merge_core(a, 0)
        if a - 1 >= 1:
            merge_minor(a - 1)
            start(rsz(a - 1))
    each_b(lambda b: start(rsx(0, b)))
    merge_minor(A - 1)
    start(rsz(A - 1))
    merge_minor(0)
    for a in range(1, A):
        arrived(rsz(a))

    def final(h):
        row = pl.ds(h, 1)
        tot = pl.ds(H + h, 1)
        ms = [lstat[row, :], stat[0, row, :]] + [zstat[j, row, :] for j in range(A - 1)]
        m = functools.reduce(jnp.maximum, ms)
        fs = [jnp.exp2((one - m) * scale) for one in ms]
        ls = [lstat[tot, :], stat[0, tot, :]] + [zstat[j, tot, :] for j in range(A - 1)]
        total = sum(f * l for f, l in zip(fs, ls))
        acc = lacc[cols(h), :] * fs[0] + part[0, cols(h), :].astype(jnp.float32) * fs[1]
        for j in range(A - 1):
            acc = acc + zpart[j, cols(h), :].astype(jnp.float32) * fs[2 + j]
        out_ref[:, cols(h)] = jnp.transpose(acc / total).astype(jnp.bfloat16)

    heads(final)

    for a in range(1, A):
        agz(a).wait_send()
        sent(rsz(a))
    for a in range(A):
        agc(a, 0).wait_send()
        sent(rsc(a, 0))

        def done(b, a=a):
            agx(a, b).wait_send()
            agc(a, b).wait_send()
            sent(rsc(a, b))
            sent(rsx(a, b))

        each_b(done)


def visit(queries_t, keys, values, req, cache_k, cache_v, table, n):
    W, T = queries_t.shape
    H = W // HD
    G = next(g for g in (6, 4, 3, 2, 1) if H % g == 0)
    A = MAJOR
    B = n // (2 * A)
    R = -(-2 * H // 8) * 8
    bf, f32 = jnp.bfloat16, jnp.float32
    dma = pltpu.SemaphoreType.DMA
    vm = pl.BlockSpec(memory_space=pltpu.VMEM)
    hbm = pl.BlockSpec(memory_space=pl.ANY)
    blocks = cache_k.shape[0]
    return pl.pallas_call(
        functools.partial(kernel, A, B, H, G),
        out_shape=jax.ShapeDtypeStruct((T, W), bf),
        in_specs=[pl.BlockSpec(memory_space=pltpu.SMEM), vm, vm, vm, vm, vm, hbm, hbm],
        out_specs=vm,
        scratch_shapes=[
            pltpu.VMEM((n, W, T), bf),
            pltpu.VMEM(cache_k.shape, bf),
            pltpu.VMEM(cache_v.shape, bf),
            pltpu.VMEM((n, W, T), bf),
            pltpu.VMEM((n, R, T), f32),
            pltpu.VMEM((A * B, W, T), bf),
            pltpu.VMEM((A * B, R, T), f32),
            pltpu.VMEM((A * (B - 1), W, T), bf),
            pltpu.VMEM((A * (B - 1), R, T), f32),
            pltpu.VMEM((A - 1, W, T), bf),
            pltpu.VMEM((A - 1, R, T), f32),
            pltpu.VMEM((W, T), f32),
            pltpu.VMEM((R, T), f32),
            dma((2,)),
            dma((A,)), dma((A,)),
            dma((A * B,)), dma((A * B,)),
            dma((A * B,)), dma((A * B,)),
            dma((A * B,)), dma((A * B,)), dma((A * B,)), dma((A * B,)),
            dma((A * (B - 1),)), dma((A * (B - 1),)), dma((A * (B - 1),)), dma((A * (B - 1),)),
            dma((A - 1,)), dma((A - 1,)), dma((A - 1,)), dma((A - 1,)),
        ],
        compiler_params=pltpu.CompilerParams(
            collective_id=0, has_side_effects=True, vmem_limit_bytes=VMEM_LIMIT
        ),
        cost_estimate=pl.CostEstimate(
            flops=4 * n * W * T * cache_k.shape[1], bytes_accessed=4 * blocks * cache_k.shape[1] * W,
            transcendentals=n * H * T * cache_k.shape[1],
        ),
    )(table, queries_t, keys, values, req[None, :], req[:, None], cache_k, cache_v)


def shards(
    q_new, k_new, v_new, q_gain, k_gain, cache_k, cache_v, new_count, prefix_blocks, block_req
):
    tokens_here = q_new.shape[0]
    width_all = q_new.shape[1] * lax.axis_size("mp")
    heads_here = q_new.shape[1] // HD
    block_len = cache_k.shape[1]
    blocks_here = cache_k.shape[0]
    slots = lax.axis_size("seq")
    device = lax.axis_index("seq")
    per_dev = new_count.shape[1]
    query_f = q_new.astype(jnp.float32)
    key_f = k_new.astype(jnp.float32)
    square_q, square_k = lax.psum(
        (jnp.sum(query_f * query_f, -1), jnp.sum(key_f * key_f, -1)), "mp"
    )
    index = jnp.arange(per_dev, dtype=jnp.int32)
    ends = jnp.sum(jnp.where(index[:, None] <= index[None, :], new_count[:, :, None], 0), 1)
    starts = ends - new_count
    order = jnp.arange(tokens_here, dtype=jnp.int32)
    my_ends, my_starts = ends[device], starts[device]
    my_prefix = prefix_blocks.reshape(slots, per_dev)[device]
    local = jnp.sum((order[:, None] >= my_ends[None, :]).astype(jnp.int32), -1)
    picker = (local[:, None] == jnp.arange(per_dev, dtype=jnp.int32)[None, :]).astype(jnp.int32)
    position = (
        jnp.sum(picker * my_prefix[None, :], -1) * block_len
        + order - jnp.sum(picker * my_starts[None, :], -1)
    )
    normed_q = query_f * lax.rsqrt(square_q / width_all + 1e-06)[:, None] * q_gain
    normed_k = key_f * lax.rsqrt(square_k / width_all + 1e-06)[:, None] * k_gain
    queries = rotate(normed_q.reshape(tokens_here, heads_here, HD), position).astype(jnp.bfloat16)
    keys = rotate(normed_k.reshape(tokens_here, heads_here, HD), position).astype(jnp.bfloat16)
    queries_t = queries.reshape(tokens_here, heads_here * HD).T
    keys = keys.reshape(tokens_here, heads_here * HD)

    minors = slots // (2 * MAJOR)
    s = jnp.arange(slots, dtype=jnp.int32)
    target = (
        ((device // (2 * minors) + s // (2 * minors)) % MAJOR) * minors
        + (device // 2 + s // 2) % minors
    ) * 2 + (device + s) % 2
    owners = lax.dynamic_slice(block_req, (device * blocks_here,), (blocks_here,))
    hit = (owners // per_dev)[None, :] == target[:, None]
    present = jnp.any(hit, 1)
    pick = jnp.sum(jnp.where(hit, jnp.arange(blocks_here, dtype=jnp.int32)[None, :], 0), 1)
    owner = jnp.sum(jnp.where(hit, owners[None, :], 0), 1)
    begin = jnp.where(present, starts.reshape(-1)[owner], 0)
    finish = jnp.where(present, ends.reshape(-1)[owner], 0)
    table = jnp.stack([pick, begin, finish]).astype(jnp.int32)
    return visit(queries_t, keys, v_new, local, cache_k, cache_v, table, slots)


def solution(mesh):
    return jax.shard_map(
        shards,
        mesh=mesh,
        in_specs=(
            P("seq", "mp"),
            P("seq", "mp"),
            P("seq", "mp"),
            P("mp"),
            P("mp"),
            P("seq", None, "mp"),
            P("seq", None, "mp"),
            P(),
            P(),
            P(),
        ),
        out_specs=P("seq", "mp"),
        check_vma=False,
    )
```

time: 357 us -> 211 us (0.59)
  the two profiles are of different devices: /device:TPU:11 before, /device:TPU:28 now
where the time goes in v1:
time: 211 us
  Pallas kernels  193 us (91%)
  local copies, waits for them, and re-layouts  6.55 us (3%)
  other arithmetic  6.32 us (3%)
  blocking collectives  4.94 us (2%)
    pallas_call x1, Pallas kernels, visit(): pl.pallas_call(functools.partial(kernel, A, B, H, G), out_shape=jax.Shape...  193 us
    psum x1, blocking collectives, shards(): lax.psum((jnp.sum(query_f * query_f, -1), jnp.sum(key_f * key_f, -1)), 'mp')  4.94 us

profile of v1, /device:TPU:28, one launch (start us, length us, event | category | flops | bytes accessed | tf_op | source)
XLA Modules:
  0.0 210.9 jit_solution(7477135223251408463)
XLA Ops:
  0.0 0.0 copy-start
  0.0 0.0 copy-start.1
  0.0 0.9 and_select_fusion.5
  0.9 0.2 compare_reduce_fusion
  1.1 0.8 select_reduce_fusion.2
  1.8 0.7 sub.38
  2.5 0.1 copy.28
  2.6 0.1 reshape.194
  2.7 0.2 fusion.4
  2.9 0.7 gather_fusion
  3.6 0.1 copy.29
  3.6 0.1 reshape.195
  3.7 0.7 gather_fusion.1
  4.4 0.6 pad_add_fusion.table
  5.0 0.0 copy-done
  5.0 0.3 copy.31
  5.3 0.0 copy-done.1
  5.3 0.0 copy-start.3
  5.3 0.3 copy.30
  5.6 0.2 fusion
  5.8 0.0 copy-start.5
  5.8 0.0 copy-start.4
  5.8 0.2 fusion.2
  6.1 4.9 %all-reduce = (f32[256]{0:T(256)S(1)}, f32[256]{0:T(256)S(1)}) all-reduce(f32[256]{0:T(256)S(1)} %fusion, f32[256]{0:T(256)S(1)} %fusion.2), channel_id=1, replica_groups=mesh['seq'=16,'mp'=2] {'mp'}, use_global_device_ids=true, to_apply=%region_5.6 | all-reduce | flops 512 | bytes 4096 | tf_op jit(solution)/shard_map/psum | solution.py:338
  11.0 0.0 copy-done.3
  11.0 0.3 fusion.3
  11.3 0.0 copy-done.5
  11.3 0.1 reshape.197
  11.4 0.2 dynamic-slice_reduce_fusion
  11.6 0.1 fusion.6
  11.7 0.0 copy-start.2
  11.7 0.1 select_reduce_fusion.1
  11.8 0.3 multiply_cosine_fusion
  12.1 0.0 copy-done.4
  12.2 0.3 fusion.1
  12.4 0.5 subtract_convert_fusion
  12.9 0.9 pad_maximum_fusion
  13.9 0.1 pad_maximum_fusion.1
  13.9 1.2 copy.32.k_ref
  15.1 0.0 copy-done.2
  15.1 0.8 copy.33.col_req
  15.9 192.9 %shard_map.100 = bf16[256,1536]{1,0:T(8,128)(2,1)} custom-call(s32[3,16]{1,0:T(4,128)} %pad_add_fusion.table, bf16[1536,256]{1,0:T(8,128)(2,1)} %bitcast.21, bf16[256,1536]{1,0:T(8,128)(2,1)} %copy.32.k_ref, bf16[256,1536]{1,0:T(8,128)(2,1)} %v_ref.1, s32[1,256]{1,0:T(1,128)} %bitcast.24, s32[256,1]{1,0:T(8,128)} %copy.33.col_req, ...), custom_call_target="tpu_custom_call" | custom-call | flops 3221225472 | bytes 12582912 | tf_op jit(solution)/shard_map/pallas_call | solution.py:288
  208.8 2.1 copy.35
  (8 shorter events, 0.1 us)
Async XLA Ops:
  0.0 5.0 %copy-start = (bf16[256,1536]{1,0:T(8,128)(2,1)S(1)}, bf16[256,1536]{1,0:T(8,128)(2,1)}, u32[]{:S(2)}) copy-start(bf16[256,1536]{1,0:T(8,128)(2,1)} %param.11) | copy-start | bytes 2359300
  0.0 5.3 %copy-start.1 = (bf16[256,1536]{1,0:T(8,128)(2,1)S(1)}, bf16[256,1536]{1,0:T(8,128)(2,1)}, u32[]{:S(2)}) copy-start(bf16[256,1536]{1,0:T(8,128)(2,1)} %param.10) | copy-start | bytes 2359300
  5.3 5.7 %copy-start.3 = (f32[1536]{0:T(1024)S(1)}, f32[1536]{0:T(1024)}, u32[]{:S(2)}) copy-start(f32[1536]{0:T(1024)} %param.14) | copy-start | bytes 18436
  5.8 5.5 %copy-start.5 = (s32[32]{0:T(128)S(1)}, s32[32]{0:T(128)}, u32[]{:S(2)}) copy-start(s32[32]{0:T(128)} %param.18) | copy-start | bytes 388
  5.8 6.3 %copy-start.4 = (f32[1536]{0:T(1024)S(1)}, f32[1536]{0:T(1024)}, u32[]{:S(2)}) copy-start(f32[1536]{0:T(1024)} %param.13) | copy-start | bytes 18436
  11.7 3.4 %copy-start.2 = (s32[256]{0:T(256)}, s32[256]{0:T(256)S(1)}, u32[]{:S(2)}) copy-start(s32[256]{0:T(256)S(1)} %fusion.6) | copy-start | bytes 3076

commit v2 on v1

--- a/solution.py
+++ b/solution.py
@@ -126,8 +126,8 @@
         each_b(lambda b: agx(a, b).start())
         agc(a, 0).start()
 
-    for a in range(1, A):
-        agz(a).start()
+    order = [0] + sorted(range(1, A), key=lambda a: (a != A // 2, a))
+    agz(order[1]).start()
     forward(0)
 
     def cols(h):
@@ -212,11 +212,18 @@
 
         each_b(body)
 
-    for a in range(A):
+    def pass_on(step):
+        if step + 1 < A:
+            agz(order[step + 1]).wait_recv()
+            forward(order[step + 1])
+            agz(order[step + 1]).wait_send()
+            if step + 2 < A:
+                agz(order[step + 2]).start()
+
+    for step, a in enumerate(order):
         unit(a, 0)
-        if a + 1 < A:
-            agz(a + 1).wait_recv()
-            forward(a + 1)
+        if step < 2:
+            pass_on(step)
 
         def far(b, a=a):
             agx(a, b).wait_recv()
@@ -231,13 +238,15 @@
                 start(rsx(a, b))
 
         each_b(near)
+        if step == A - 1:
+            each_b(lambda b: start(rsx(0, b)))
         merge_core(a, 0)
-        if a - 1 >= 1:
-            merge_minor(a - 1)
-            start(rsz(a - 1))
-    each_b(lambda b: start(rsx(0, b)))
-    merge_minor(A - 1)
-    start(rsz(A - 1))
+        if step >= 2:
+            pass_on(step)
+            merge_minor(order[step - 1])
+            start(rsz(order[step - 1]))
+    merge_minor(order[-1])
+    start(rsz(order[-1]))
     merge_minor(0)
     for a in range(1, A):
         arrived(rsz(a))
@@ -258,7 +267,6 @@
     heads(final)
 
     for a in range(1, A):
-        agz(a).wait_send()
         sent(rsz(a))
     for a in range(A):
         agc(a, 0).wait_send()

time: 211 us -> 192 us (0.910); the launches traced: 211 us -> 189 us
  Pallas kernels: 193 us -> 171 us
    pallas_call x1, Pallas kernels: 193 us -> 171 us  [visit(): pl.pallas_call(functools.partial(kernel, A, B, H, G), out_shape=jax.Shape...]
where the time goes in v2:
time: 192 us; the launch traced here: 189 us
  Pallas kernels  171 us (89%)
  local copies, waits for them, and re-layouts  6.55 us (3%)
  other arithmetic  6.32 us (3%)
  blocking collectives  4.94 us (3%)
    pallas_call x1, Pallas kernels, visit(): pl.pallas_call(functools.partial(kernel, A, B, H, G), out_shape=jax.Shape...  171 us
    psum x1, blocking collectives, shards(): lax.psum((jnp.sum(query_f * query_f, -1), jnp.sum(key_f * key_f, -1)), 'mp')  4.94 us

profile of v2, /device:TPU:28, one launch (start us, length us, event | category | flops | bytes accessed | tf_op | source)
XLA Modules:
  0.0 188.7 jit_solution(4735034557544157982)
XLA Ops:
  0.0 0.0 copy-start
  0.0 0.0 copy-start.1
  0.0 0.9 and_select_fusion.5
  0.9 0.2 compare_reduce_fusion
  1.1 0.8 select_reduce_fusion.2
  1.8 0.7 sub.38
  2.5 0.1 copy.28
  2.6 0.1 reshape.194
  2.7 0.2 fusion.4
  2.9 0.7 gather_fusion
  3.6 0.1 copy.29
  3.6 0.1 reshape.195
  3.7 0.7 gather_fusion.1
  4.4 0.6 pad_add_fusion.table
  5.0 0.0 copy-done
  5.0 0.3 copy.31
  5.3 0.0 copy-done.1
  5.3 0.0 copy-start.3
  5.3 0.3 copy.30
  5.6 0.2 fusion
  5.8 0.0 copy-start.5
  5.8 0.0 copy-start.4
  5.8 0.2 fusion.2
  6.1 4.9 %all-reduce = (f32[256]{0:T(256)S(1)}, f32[256]{0:T(256)S(1)}) all-reduce(f32[256]{0:T(256)S(1)} %fusion, f32[256]{0:T(256)S(1)} %fusion.2), channel_id=1, replica_groups=mesh['seq'=16,'mp'=2] {'mp'}, use_global_device_ids=true, to_apply=%region_5.6 | all-reduce | flops 512 | bytes 4096 | tf_op jit(solution)/shard_map/psum | solution.py:346
  11.0 0.0 copy-done.3
  11.0 0.3 fusion.3
  11.3 0.0 copy-done.5
  11.3 0.1 reshape.197
  11.4 0.2 dynamic-slice_reduce_fusion
  11.6 0.1 fusion.6
  11.7 0.0 copy-start.2
  11.7 0.1 select_reduce_fusion.1
  11.8 0.3 multiply_cosine_fusion
  12.1 0.0 copy-done.4
  12.2 0.3 fusion.1
  12.4 0.5 subtract_convert_fusion
  12.9 0.9 pad_maximum_fusion
  13.9 0.1 pad_maximum_fusion.1
  13.9 1.2 copy.32.k_ref
  15.1 0.0 copy-done.2
  15.1 0.8 copy.33.col_req
  15.9 170.8 %shard_map.100 = bf16[256,1536]{1,0:T(8,128)(2,1)} custom-call(s32[3,16]{1,0:T(4,128)} %pad_add_fusion.table, bf16[1536,256]{1,0:T(8,128)(2,1)} %bitcast.21, bf16[256,1536]{1,0:T(8,128)(2,1)} %copy.32.k_ref, bf16[256,1536]{1,0:T(8,128)(2,1)} %v_ref.1, s32[1,256]{1,0:T(1,128)} %bitcast.24, s32[256,1]{1,0:T(8,128)} %copy.33.col_req, ...), custom_call_target="tpu_custom_call" | custom-call | flops 3221225472 | bytes 12582912 | tf_op jit(solution)/shard_map/pallas_call | solution.py:296
  186.7 2.1 %copy.35 = bf16[256,1536]{1,0:T(8,128)(2,1)} copy(bf16[256,1536]{1,0:T(8,128)(2,1)} %shard_map.100) | data formatting | bytes 1572864
  (8 shorter events, 0.1 us)
Async XLA Ops:
  0.0 5.0 %copy-start = (bf16[256,1536]{1,0:T(8,128)(2,1)S(1)}, bf16[256,1536]{1,0:T(8,128)(2,1)}, u32[]{:S(2)}) copy-start(bf16[256,1536]{1,0:T(8,128)(2,1)} %param.11) | copy-start | bytes 2359300
  0.0 5.3 %copy-start.1 = (bf16[256,1536]{1,0:T(8,128)(2,1)S(1)}, bf16[256,1536]{1,0:T(8,128)(2,1)}, u32[]{:S(2)}) copy-start(bf16[256,1536]{1,0:T(8,128)(2,1)} %param.10) | copy-start | bytes 2359300
  5.3 5.7 %copy-start.3 = (f32[1536]{0:T(1024)S(1)}, f32[1536]{0:T(1024)}, u32[]{:S(2)}) copy-start(f32[1536]{0:T(1024)} %param.14) | copy-start | bytes 18436
  5.8 5.5 %copy-start.5 = (s32[32]{0:T(128)S(1)}, s32[32]{0:T(128)}, u32[]{:S(2)}) copy-start(s32[32]{0:T(128)} %param.18) | copy-start | bytes 388
  5.8 6.3 %copy-start.4 = (f32[1536]{0:T(1024)S(1)}, f32[1536]{0:T(1024)}, u32[]{:S(2)}) copy-start(f32[1536]{0:T(1024)} %param.13) | copy-start | bytes 18436
  11.7 3.4 %copy-start.2 = (s32[256]{0:T(256)}, s32[256]{0:T(256)S(1)}, u32[]{:S(2)}) copy-start(s32[256]{0:T(256)S(1)} %fusion.6) | copy-start | bytes 3076
